TPU v7x, 32 devices: a whole 2x2x4 slice. The times are simulated.
32 devices in a mesh: rows: 8 (over z, y), snaps: 4 (over x, core).
Axes of the slice: x: 2, y: 2, z: 4, core: 2. Of those that a mesh axis runs over, the one named last changes fastest.
Arguments:
- stress: float32 [131072, 1024], P('rows', 'snaps'), may hold values from -80 to 80
- sketch: float32 [64, 1024], P(None, 'snaps'), may hold values from -0.1875 to 0.1875
Outputs:
- basis: float32 [64, 131072], P(None, ('rows', 'snaps'))
- coeffs: float32 [64, 1024], P(None, 'snaps')
- spectrum: float32 [64, 64], replicated
All inputs are finite; a program needn't handle non-finite values.
Results may differ from a plain program's by a relative error of at most 0.0015.
Values sent between devices are 32-bit elements; how exact they have to be, the bound alone decides.
A program may use at most 128 MiB of HBM per device.

v0:
```python
import math

import jax
import jax.numpy as jnp
from jax import lax
from jax.sharding import PartitionSpec as P


def product(left_m, right_m, left_dim, right_dim):
    return lax.dot_general(
        left_m,
        right_m,
        (((left_dim,), (right_dim,)), ((), ())),
        precision=lax.Precision.HIGHEST,
        preferred_element_type=jnp.float32,
    )


def inverse_factor(gram_total):
    lower = jnp.linalg.cholesky(gram_total)
    ident = jnp.eye(gram_total.shape[0], dtype=gram_total.dtype)
    return lax.linalg.triangular_solve(lower, ident, left_side=True, lower=True)


def section_whole(panel, stress):
    factor = inverse_factor(lax.psum(product(panel, panel, 1, 1), "rows"))
    basis = product(factor, panel, 1, 0)
    coeffs = lax.psum(product(basis, stress, 1, 0), "rows")
    return (basis, coeffs)


def on_device(stress, sketch):
    rows_dev = stress.shape[0]
    groups = lax.axis_size("snaps")
    share = rows_dev // groups
    operand = sketch
    basis = None
    for turn in range(2):
        partial_value = product(operand, stress, 1, 1)
        panel = lax.psum(partial_value, "snaps")
        basis, operand = section_whole(panel, stress)
    basis = lax.dynamic_slice_in_dim(basis, lax.axis_index("snaps") * share, share, 1)
    scale = math.sqrt(float(rows_dev * lax.axis_size("rows")))
    batch_total = operand.shape[1] * groups
    spectrum = lax.psum(product(operand, operand, 1, 1), "snaps") / batch_total
    return (basis * scale, operand, spectrum)


def solution(mesh):
    placed = (P("rows", "snaps"), P(None, "snaps"))
    return jax.shard_map(
        on_device,
        mesh=mesh,
        in_specs=placed,
        out_specs=(P(None, ("rows", "snaps")), P(None, "snaps"), P()),
        check_vma=False,
    )
```

profile of v0, /device:TPU:0, one launch (start us, length us, event | category | flops | bytes accessed | tf_op | source)
XLA Modules:
  0.0 522.6 jit_solution(17021512674975102727)
XLA Ops:
  7.2 0.8 copy-done
  8.0 20.6 %fusion.12 = f32[64,16384]{1,0:T(8,128)} fusion(f32[64,256]{1,0:T(8,128)S(1)} %copy-done, f32[16384,256]{1,0:T(8,128)} %param.5), kind=kOutput, calls=%fused_computation.23 | convolution fusion | flops 3221225472 | bytes 21037056 | tf_op jit(solution)/shard_map/dot_general | solution.py:10
  28.7 88.3 %all-reduce.5.cloned.1.call-done = f32[64,16384]{1,0:T(8,128)} async-done(((f32[64,16384]{1,0:T(8,128)}), f32[64,16384]{1,0:T(8,128)}) %all-reduce.5.cloned.1.call-update) | async-done | bytes 4194320 | tf_op jit(solution)/shard_map/psum | solution.py:40
  117.0 6.9 %fusion.13 = f32[64,64]{0,1:T(8,128)S(1)} fusion(f32[64,16384]{1,0:T(8,128)} %all-reduce.5.cloned.1.call-done), kind=kOutput, calls=%fused_computation.24 | convolution fusion | flops 805306368 | bytes 4210688 | tf_op jit(solution)/shard_map/dot_general | solution.py:10
  124.0 37.2 %psum.50 = f32[64,64]{0,1:T(8,128)S(1)} all-reduce(f32[64,64]{0,1:T(8,128)S(1)} %fusion.13), channel_id=1, replica_groups=mesh['rows'=8,'snaps'=4] {'rows'}, use_global_device_ids=true, to_apply=%region_1.0 | all-reduce | flops 4096 | bytes 32768 | tf_op jit(solution)/shard_map/psum | solution.py:26
  161.2 5.8 %cholesky.44 = f32[64,64]{1,0:T(8,128)S(1)} custom-call(f32[64,64]{1,0:T(8,128)S(1)} %fusion.9), custom_call_target="Cholesky" | custom-call | tf_op jit(solution)/shard_map/jit(cholesky)/cholesky | solution.py:20
  167.1 0.6 compare_reduce_fusion.1
  167.7 0.7 fusion.4
  168.4 4.9 custom-call.6
  173.3 0.3 fusion.2
  173.5 5.5 %fusion.14 = f32[64,16384]{1,0:T(8,128)S(1)} fusion(f32[64,64]{1,0:T(8,128)S(1)} %fusion.2, f32[64,16384]{1,0:T(8,128)} %all-reduce.5.cloned.1.call-done), kind=kOutput, calls=%fused_computation.25 | convolution fusion | flops 805306368 | bytes 8404992 | tf_op jit(solution)/shard_map/dot_general | solution.py:10
  179.0 11.6 %fusion.15 = f32[64,256]{1,0:T(8,128)} fusion(f32[64,16384]{1,0:T(8,128)S(1)} %fusion.14, f32[16384,256]{1,0:T(8,128)} %param.5), kind=kOutput, calls=%fused_computation.26 | convolution fusion | flops 3221225472 | bytes 21037056 | tf_op jit(solution)/shard_map/dot_general | solution.py:10
  190.6 0.3 all-reduce.9.cloned.1.call-start
  190.9 64.8 %all-reduce.7.cloned.1.call-done = f32[64,256]{1,0:T(8,128)} async-done(((f32[64,256]{1,0:T(8,128)}), f32[64,256]{1,0:T(8,128)}) %all-reduce.7.cloned.1.call-update) | async-done | bytes 65552 | tf_op jit(solution)/shard_map/psum | solution.py:28
  255.7 20.6 %fusion.16 = f32[64,16384]{1,0:T(8,128)} fusion(f32[64,256]{1,0:T(8,128)} %all-reduce.7.cloned.1.call-done, f32[16384,256]{1,0:T(8,128)} %param.5), kind=kOutput, calls=%fused_computation.27 | convolution fusion | flops 3221225472 | bytes 21037056 | tf_op jit(solution)/shard_map/dot_general | solution.py:10
  276.4 85.5 %all-reduce.9.cloned.1.call-done = f32[64,16384]{1,0:T(8,128)} async-done(((f32[64,16384]{1,0:T(8,128)}), f32[64,16384]{1,0:T(8,128)}) %all-reduce.9.cloned.1.call-update) | async-done | bytes 4194320 | tf_op jit(solution)/shard_map/psum | solution.py:40
  361.9 6.9 %fusion.17 = f32[64,64]{0,1:T(8,128)S(1)} fusion(f32[64,16384]{1,0:T(8,128)} %all-reduce.9.cloned.1.call-done), kind=kOutput, calls=%fused_computation.28 | convolution fusion | flops 805306368 | bytes 4210688 | tf_op jit(solution)/shard_map/dot_general | solution.py:10
  368.9 37.1 %psum.53 = f32[64,64]{0,1:T(8,128)S(1)} all-reduce(f32[64,64]{0,1:T(8,128)S(1)} %fusion.17), channel_id=1, replica_groups=mesh['rows'=8,'snaps'=4] {'rows'}, use_global_device_ids=true, to_apply=%region_6.9 | all-reduce | flops 4096 | bytes 32768 | tf_op jit(solution)/shard_map/psum | solution.py:26
  406.1 5.8 %cholesky.55 = f32[64,64]{1,0:T(8,128)S(1)} custom-call(f32[64,64]{1,0:T(8,128)S(1)} %fusion.7), custom_call_target="Cholesky" | custom-call | tf_op jit(solution)/shard_map/jit(cholesky)/cholesky | solution.py:20
  412.0 0.6 compare_reduce_fusion
  412.7 0.7 fusion.5
  413.3 4.9 custom-call.7
  418.2 0.3 fusion
  418.5 5.5 %fusion.18 = f32[64,16384]{1,0:T(8,128)S(1)} fusion(f32[64,64]{1,0:T(8,128)S(1)} %fusion, f32[64,16384]{1,0:T(8,128)} %all-reduce.9.cloned.1.call-done), kind=kOutput, calls=%fused_computation.29 | convolution fusion | flops 805306368 | bytes 8404992 | tf_op jit(solution)/shard_map/dot_general | solution.py:10
  423.9 1.9 copy-done.1
  425.9 11.6 %fusion.19 = f32[64,256]{1,0:T(8,128)} fusion(f32[64,16384]{1,0:T(8,128)S(1)} %fusion.18, f32[16384,256]{1,0:T(8,128)} %param.5), kind=kOutput, calls=%fused_computation.30 | convolution fusion | flops 3221225472 | bytes 21037056 | tf_op jit(solution)/shard_map/dot_general | solution.py:10
  437.5 2.3 dynamic-slice_multiply_fusion
  439.8 62.8 %all-reduce.11.cloned.1.call-done = f32[64,256]{1,0:T(8,128)} async-done(((f32[64,256]{1,0:T(8,128)}), f32[64,256]{1,0:T(8,128)}) %all-reduce.11.cloned.1.call-update) | async-done | bytes 65552 | tf_op jit(solution)/shard_map/psum | solution.py:28
  502.5 1.1 fusion.20
  503.7 10.3 %psum.55 = f32[64,64]{1,0:T(8,128)S(1)} all-reduce(f32[64,64]{1,0:T(8,128)S(1)} %fusion.20), channel_id=1, replica_groups=mesh['rows'=8,'snaps'=4] {'snaps'}, use_global_device_ids=true, to_apply=%region_8.11 | all-reduce | flops 4096 | bytes 32768 | tf_op jit(solution)/shard_map/psum | solution.py:45
  513.9 0.6 broadcast_multiply_fusion
  514.6 1.5 copy.15
  (15 shorter events, 0.4 us)
Async XLA Ops:
  7.2 0.8 copy-start
  7.2 109.8 %all-reduce.5.cloned.1.call-start = ((), (), s32[]{:S(2)}) async-start(), calls=%async_computation | async-start | bytes 8388608 | tf_op jit(solution)/shard_map/psum | solution.py:40
  28.7 227.1 %all-reduce.7.cloned.1.call-start = ((), (), s32[]{:S(2)}) async-start(), calls=%async_computation.1 | async-start | bytes 131072 | tf_op jit(solution)/shard_map/psum | solution.py:28
  190.6 171.3 %all-reduce.9.cloned.1.call-start = ((), (), s32[]{:S(2)}) async-start(), calls=%async_computation.2 | async-start | bytes 8388608 | tf_op jit(solution)/shard_map/psum | solution.py:40
  276.4 226.2 %all-reduce.11.cloned.1.call-start = ((), (), s32[]{:S(2)}) async-start(), calls=%async_computation.3 | async-start | bytes 131072 | tf_op jit(solution)/shard_map/psum | solution.py:28
  423.9 1.9 copy-start.1
Sparse Core Ops, SparseCore 0:
  28.8 88.1 all-reduce.4
  190.8 64.9 all-reduce.6
  276.5 85.4 all-reduce.8
  437.6 64.9 all-reduce.10
where the time goes:
time: 523 us
  waiting for transfers between devices  301 us (58%)
  matrix products  90.8 us (17%)
  blocking collectives  84.6 us (16%)
  other arithmetic  27.1 us (5%)
  between operations  13.9 us (3%)
    psum x2, waiting for transfers between devices, on_device(): panel = lax.psum(partial_value, 'snaps')  174 us
    psum x2, waiting for transfers between devices, section_whole(): coeffs = lax.psum(product(basis, stress, 1, 0), 'rows')  128 us
    dot_general x9, matrix products, product(): lax.dot_general(left_m, right_m, (((left_dim,), (right_dim,)), ((), ())),...  90.3 us
    psum x2, blocking collectives, section_whole(): factor = inverse_factor(lax.psum(product(panel, panel, 1, 1), 'rows'))  74.3 us
    another operation x6, other arithmetic, inverse_factor(): lower = jnp.linalg.cholesky(gram_total)  13 us
    another operation x4, other arithmetic, inverse_factor(): return lax.linalg.triangular_solve(lower, ident, left_side=True, lower=True)  11.1 us
  transfers between devices with their start and end apart: 4, of which 4 were waited for; matrix products, arithmetic and copies ran while one was open for 0% of the time, Pallas kernels for 0%

commit v1 on v0

v1 whole, which is shorter than its diff:
```python
import functools
import math

import jax
import jax.numpy as jnp
from jax import lax
from jax.experimental import pallas as pl
from jax.experimental.pallas import tpu as pltpu
from jax.sharding import PartitionSpec as P

MESH = pl.DeviceIdType.MESH
F32 = jnp.float32
BF16 = jnp.bfloat16
CHUNK = 1024
HALF = CHUNK // 2
SLOTS = 4
PIECE = 128
TURNS = 2


def dot(left_m, right_m, left_dim, right_dim, precision=None):
    return lax.dot_general(
        left_m,
        right_m,
        (((left_dim,), (right_dim,)), ((), ())),
        precision=precision,
        preferred_element_type=F32,
    )


def dot_full(left_m, right_m, left_dim, right_dim):
    return dot(left_m, right_m, left_dim, right_dim, lax.Precision.HIGHEST)


def split(value):
    high = value.astype(BF16)
    low = (value - high.astype(F32)).astype(BF16)
    return high, low


def inverse_factor(gram):
    k = gram.shape[0]
    line = lax.broadcasted_iota(jnp.int32, (k, k), 0)
    lane = lax.broadcasted_iota(jnp.int32, (k, k), 1)
    wide_line = lax.broadcasted_iota(jnp.int32, (k, 2 * k), 0)
    ident = jnp.where(line == lane, 1.0, 0.0).astype(F32)
    table = jnp.concatenate([gram, ident], axis=1)
    for j in range(k - 1):
        row = table[j : j + 1, :]
        row = row / row[:, j : j + 1]
        column = jnp.where(wide_line > j, table[:, j : j + 1], 0.0)
        table = table - column * row
    diag = jnp.sum(jnp.where(line == lane, table[:, :k], 0.0), axis=1, keepdims=True)
    return table[:, k:] / jnp.sqrt(diag)


def kernel(
    ranks, scale, batch_total,
    stress, sketch, basis_out, coeffs_out, spectrum_out,
    stage, high, low, operand, part, got1, summed, got2, panel,
    acc, spread, landed, total, full, spect,
    stage_sem, send1, recv1, send2, recv2, send3, recv3,
    rs_send, rs_recv, ag_send, ag_recv, sp_send, sp_recv,
):
    groups = 4
    k = sketch.shape[0]
    width = stress.shape[1]
    chunks = part.shape[0]
    lines = k // ranks
    me_row = lax.axis_index("rows")
    me = lax.axis_index("snaps")
    mine = me % 2
    core = me + 1 - 2 * mine
    chip = (me + 2) % groups

    def load(c):
        slot = c % SLOTS
        return pltpu.make_async_copy(
            stress.at[pl.ds(c * CHUNK, CHUNK), :], stage.at[slot], stage_sem.at[slot]
        )

    for c in range(SLOTS):
        load(c).start()

    barrier = pltpu.get_barrier_semaphore()
    for d in range(1, ranks):
        pl.semaphore_signal(
            barrier, inc=1, device_id={"rows": (me_row + d) % ranks}, device_id_type=MESH
        )
    for d in range(1, groups):
        pl.semaphore_signal(
            barrier, inc=1, device_id={"snaps": (me + d) % groups}, device_id_type=MESH
        )

    def remote(src, dst, s_sem, r_sem, device):
        return pltpu.make_async_remote_copy(
            src_ref=src, dst_ref=dst, send_sem=s_sem, recv_sem=r_sem,
            device_id=device, device_id_type=MESH,
        )

    def hop1(t, c):
        return remote(
            part.at[c, 1 - mine], got1.at[t, c], send1.at[t, c], recv1.at[t, c], {"snaps": core}
        )

    def hop2(t, c):
        return remote(summed.at[c], got2.at[t, c], send2.at[t, c], recv2.at[t, c], {"snaps": chip})

    def hop3(t, c):
        return remote(
            panel.at[t, c, mine], panel.at[t, c, mine], send3.at[t, c], recv3.at[t, c],
            {"snaps": core},
        )

    def scatter(t, d):
        to = (me_row + d) % ranks
        return remote(
            spread.at[to], landed.at[t, d], rs_send.at[t, d], rs_recv.at[t, d], {"rows": to}
        )

    def gather(t, d):
        to = (me_row + d) % ranks
        return remote(
            total.at[t], full.at[t, me_row], ag_send.at[t, d], ag_recv.at[t, d], {"rows": to}
        )

    def share_spectrum(d):
        return remote(
            spect.at[0], spect.at[d], sp_send.at[d], sp_recv.at[d], {"snaps": (me + d) % groups}
        )

    def set_operand(value):
        h, l = split(value)
        operand[0:k, :] = h
        operand[k : 2 * k, :] = l

    def convert(c):
        slot = c % SLOTS
        load(c).wait()

        def body(p, carry):
            h, l = split(stage[slot, pl.ds(p * PIECE, PIECE), :])
            at = pl.ds(c * CHUNK + p * PIECE, PIECE)
            high[at, :] = h
            low[at, :] = l
            return carry

        lax.fori_loop(0, CHUNK // PIECE, body, 0)

        @pl.when(c + SLOTS < chunks)
        def _():
            load(c + SLOTS).start()

    def project(t, c):
        if t == 0:
            convert(c)
        for h in range(2):
            at = pl.ds(c * CHUNK + h * HALF, HALF)
            both = dot(operand[...], high[at, :], 1, 1)
            rest = dot(operand[0:k, :], low[at, :], 1, 1)
            part[c, h] = both[0:k] + (both[k : 2 * k] + rest)

    def add_cores(t, c):
        hop1(t, c).wait_recv()
        summed[c] = part[c, mine] + got1[t, c]
        hop2(t, c).start()

    def add_chips(t, c):
        hop2(t, c).wait_recv()
        panel[t, c, mine] = summed[c] + got2[t, c]
        hop3(t, c).start()

    def accumulate(t, c):
        hop3(t, c).wait_recv()
        for h in range(2):
            value = panel[t, c, h]
            hi, lo = split(value)
            at = pl.ds(c * CHUNK + h * HALF, HALF)
            both = dot(jnp.concatenate([hi, lo], axis=0), high[at, :], 1, 0)
            rest = dot(hi, low[at, :], 1, 0)
            acc[:, 0:width] += both[0:k] + (both[k : 2 * k] + rest)
            acc[:, width : width + k] += dot_full(value, value, 1, 1)

    set_operand(sketch[...])
    factor = None
    sums = None
    for t in range(TURNS):
        acc[...] = jnp.zeros_like(acc)
        project(t, 0)
        if t == 0:
            pl.semaphore_wait(barrier, ranks - 1 + groups - 1)
        hop1(t, 0).start()

        def first(c, carry, t=t):
            project(t, c)
            hop1(t, c).start()
            add_cores(t, c - 1)
            return carry

        lax.fori_loop(1, chunks, first, 0)
        add_cores(t, chunks - 1)
        add_chips(t, 0)

        def second(c, carry, t=t):
            add_chips(t, c)
            accumulate(t, c - 1)
            return carry

        lax.fori_loop(1, chunks, second, 0)
        accumulate(t, chunks - 1)

        for r in range(ranks):
            spread[r] = acc[r * lines : (r + 1) * lines, :]
        for d in range(1, ranks):
            scatter(t, d).start()
        value = spread[me_row]
        for d in range(1, ranks):
            scatter(t, d).wait_recv()
            value = value + landed[t, d]
        total[t] = value
        full[t, me_row] = value
        for d in range(1, ranks):
            gather(t, d).start()

        def drain(c, carry, t=t):
            hop1(t, c).wait_send()
            hop2(t, c).wait_send()
            hop3(t, c).wait_send()
            return carry

        lax.fori_loop(0, chunks, drain, 0)
        for d in range(1, ranks):
            scatter(t, d).wait_send()
            gather(t, d).wait_recv()
        for d in range(1, ranks):
            gather(t, d).wait_send()
        for r in range(ranks):
            acc[r * lines : (r + 1) * lines, :] = full[t, r]
        factor = inverse_factor(acc[:, width : width + k])
        sums = dot_full(factor, acc[:, 0:width], 1, 0)
        if t + 1 < TURNS:
            set_operand(sums)

    coeffs_out[...] = sums
    own = dot_full(sums, sums, 1, 1)
    spect[0] = own
    for d in range(1, groups):
        share_spectrum(d).start()
    per = chunks // groups
    scaled = factor * scale
    for i in range(per):
        for h in range(2):
            at = (i * 2 + h) * HALF
            basis_out[:, at : at + HALF] = dot_full(scaled, panel[TURNS - 1, me * per + i, h], 1, 0)
    value = None
    for d in range(1, groups):
        share_spectrum(d).wait()
    a = spect[0] + spect[2]
    b = spect[1] + spect[3]
    spectrum_out[...] = (a + b) / batch_total


def on_device(stress, sketch):
    rows_dev, width = stress.shape
    k = sketch.shape[0]
    groups = lax.axis_size("snaps")
    ranks = lax.axis_size("rows")
    share = rows_dev // groups
    chunks = rows_dev // CHUNK
    lines = k // ranks
    wide = width + 128
    scale = math.sqrt(float(rows_dev * ranks))
    vmem = pl.BlockSpec(memory_space=pltpu.VMEM)
    dma = pltpu.SemaphoreType.DMA
    return pl.pallas_call(
        functools.partial(kernel, ranks, scale, float(width * groups)),
        out_shape=(
            jax.ShapeDtypeStruct((k, share), F32),
            jax.ShapeDtypeStruct((k, width), F32),
            jax.ShapeDtypeStruct((k, k), F32),
        ),
        in_specs=[pl.BlockSpec(memory_space=pl.ANY), vmem],
        out_specs=(vmem, vmem, vmem),
        scratch_shapes=[
            pltpu.VMEM((SLOTS, CHUNK, width), F32),
            pltpu.VMEM((rows_dev, width), BF16),
            pltpu.VMEM((rows_dev, width), BF16),
            pltpu.VMEM((2 * k, width), BF16),
            pltpu.VMEM((chunks, 2, k, HALF), F32),
            pltpu.VMEM((TURNS, chunks, k, HALF), F32),
            pltpu.VMEM((chunks, k, HALF), F32),
            pltpu.VMEM((TURNS, chunks, k, HALF), F32),
            pltpu.VMEM((TURNS, chunks, 2, k, HALF), F32),
            pltpu.VMEM((k, wide), F32),
            pltpu.VMEM((ranks, lines, wide), F32),
            pltpu.VMEM((TURNS, ranks, lines, wide), F32),
            pltpu.VMEM((TURNS, lines, wide), F32),
            pltpu.VMEM((TURNS, ranks, lines, wide), F32),
            pltpu.VMEM((groups, k, k), F32),
            dma((SLOTS,)),
            dma((TURNS, chunks)),
            dma((TURNS, chunks)),
            dma((TURNS, chunks)),
            dma((TURNS, chunks)),
            dma((TURNS, chunks)),
            dma((TURNS, chunks)),
            dma((TURNS, ranks)),
            dma((TURNS, ranks)),
            dma((TURNS, ranks)),
            dma((TURNS, ranks)),
            dma((groups,)),
            dma((groups,)),
        ],
        compiler_params=pltpu.CompilerParams(
            collective_id=0, has_side_effects=True, vmem_limit_bytes=58 * 1024 * 1024
        ),
        cost_estimate=pl.CostEstimate(
            flops=24 * rows_dev * width * k, bytes_accessed=rows_dev * width * 4, transcendentals=0
        ),
    )(stress, sketch)


def solution(mesh):
    placed = (P("rows", "snaps"), P(None, "snaps"))
    return jax.shard_map(
        on_device,
        mesh=mesh,
        in_specs=placed,
        out_specs=(P(None, ("rows", "snaps")), P(None, "snaps"), P()),
        check_vma=False,
    )
```

time: 523 us -> 149 us (0.28)
  waiting for transfers between devices: 301 us -> 0 us
  Pallas kernels: 0 us -> 143 us
  matrix products: 90.8 us -> 0 us
  blocking collectives: 84.6 us -> 0 us
  other arithmetic: 27.1 us -> 0 us
  between operations: 13.9 us -> 0.64 us
    psum x4 -> x0, waiting for transfers between devices: 301 us -> none  [the longest x2 174 us: on_device(): panel = lax.psum(partial_value, 'snaps')]
    pallas_call x0 -> x1, Pallas kernels: none -> 143 us  [on_device(): pl.pallas_call(functools.partial(kernel, ranks, scale, float(width * grou...]
    dot_general x9 -> x0, matrix products: 90.3 us -> none  [product(): lax.dot_general(left_m, right_m, (((left_dim,), (right_dim,)), ((), ())),...]
    psum x3 -> x0, blocking collectives: 84.6 us -> none  [the longest x2 74.3 us: section_whole(): factor = inverse_factor(lax.psum(product(panel, panel, 1, 1), 'rows'))]
    another operation x10 -> x0, other arithmetic: 24.1 us -> none  [the longest x6 13 us: inverse_factor(): lower = jnp.linalg.cholesky(gram_total)]
  transfers between devices with their start and end apart: 4 -> 0, of which waited for: 4 -> 0; matrix products, arithmetic and copies ran while one was open for 0% -> 0% of each run, Pallas kernels for 0% -> 0%
where the time goes in v1:
time: 149 us
  Pallas kernels  143 us (96%)
  local copies, waits for them, and re-layouts  5.12 us (3%)
    pallas_call x1, Pallas kernels, on_device(): pl.pallas_call(functools.partial(kernel, ranks, scale, float(width * grou...  143 us
    unnamed x3, local copies, waits for them, and re-layouts  5.12 us

profile of v1, /device:TPU:0, one launch (start us, length us, event | category | flops | bytes accessed | tf_op | source)
XLA Modules:
  0.0 148.6 jit_solution(13220029254833596175)
XLA Ops:
  0.6 142.8 %shard_map.49 = (f32[64,4096]{1,0:T(8,128)}, f32[64,256]{1,0:T(8,128)}, f32[64,64]{1,0:T(8,128)}) custom-call(f32[16384,256]{1,0:T(8,128)} %stress.1, f32[64,256]{1,0:T(8,128)} %sketch.1), custom_call_target="tpu_custom_call" | custom-call | flops 6442450944 | bytes 16777216 | tf_op jit(solution)/shard_map/pallas_call | solution.py:275
  143.5 2.3 %copy.8 = f32[64,4096]{1,0:T(8,128)} copy(f32[64,4096]{1,0:T(8,128)} %get-tuple-element.6) | data formatting | bytes 2097152
  145.7 1.5 copy.9
  147.2 1.4 copy.10

commit v2 on v1

--- a/solution.py
+++ b/solution.py
@@ -55,12 +55,12 @@
 
 
 def kernel(
-    ranks, scale, batch_total,
-    stress, sketch, basis_out, coeffs_out, spectrum_out,
+    ranks, batch_total,
+    stress, sketch, share_out, factor_out, coeffs_out, spectrum_out,
     stage, high, low, operand, part, got1, summed, got2, panel,
-    acc, spread, landed, total, full, spect,
-    stage_sem, send1, recv1, send2, recv2, send3, recv3,
-    rs_send, rs_recv, ag_send, ag_recv, sp_send, sp_recv,
+    acc, spread, landed, total, full, spect, gram, grams, acc_gram, factor, whole,
+    stage_sem, share_sem, send1, recv1, send2, recv2, send3, recv3,
+    rs_send, rs_recv, ag_send, ag_recv, sp_send, sp_recv, gr_send, gr_recv,
 ):
     groups = 4
     k = sketch.shape[0]
@@ -124,10 +124,19 @@
             total.at[t], full.at[t, me_row], ag_send.at[t, d], ag_recv.at[t, d], {"rows": to}
         )
 
+    def give_gram(d):
+        return remote(
+            gram, grams.at[me_row], gr_send.at[d], gr_recv.at[d], {"rows": (me_row + d) % ranks}
+        )
+
     def share_spectrum(d):
         return remote(
             spect.at[0], spect.at[d], sp_send.at[d], sp_recv.at[d], {"snaps": (me + d) % groups}
         )
+
+    def share_copy():
+        per = chunks // groups
+        return pltpu.make_async_copy(whole.at[pl.ds(me * per, per)], share_out, share_sem)
 
     def set_operand(value):
         h, l = split(value)
@@ -174,6 +183,9 @@
         hop3(t, c).wait_recv()
         for h in range(2):
             value = panel[t, c, h]
+            if t > 0:
+                value = dot_full(factor[...], value, 1, 0)
+                whole[c, h] = value
             hi, lo = split(value)
             at = pl.ds(c * CHUNK + h * HALF, HALF)
             both = dot(jnp.concatenate([hi, lo], axis=0), high[at, :], 1, 0)
@@ -182,8 +194,6 @@
             acc[:, width : width + k] += dot_full(value, value, 1, 1)
 
     set_operand(sketch[...])
-    factor = None
-    sums = None
     for t in range(TURNS):
         acc[...] = jnp.zeros_like(acc)
         project(t, 0)
@@ -199,6 +209,8 @@
 
         lax.fori_loop(1, chunks, first, 0)
         add_cores(t, chunks - 1)
+        if t > 0:
+            factor[...] = inverse_factor(acc_gram[...])
         add_chips(t, 0)
 
         def second(c, carry, t=t):
@@ -209,10 +221,23 @@
         lax.fori_loop(1, chunks, second, 0)
         accumulate(t, chunks - 1)
 
+        last = t == TURNS - 1
+        if last:
+            own_gram = acc[:, width : width + k]
+            gram[...] = own_gram
+            grams[me_row] = own_gram
+            for d in range(1, ranks):
+                give_gram(d).start()
         for r in range(ranks):
             spread[r] = acc[r * lines : (r + 1) * lines, :]
         for d in range(1, ranks):
             scatter(t, d).start()
+        if last:
+            for d in range(1, ranks):
+                give_gram(d).wait_recv()
+            gram_total = grams[0]
+            for r in range(1, ranks):
+                gram_total = gram_total + grams[r]
         value = spread[me_row]
         for d in range(1, ranks):
             scatter(t, d).wait_recv()
@@ -221,6 +246,9 @@
         full[t, me_row] = value
         for d in range(1, ranks):
             gather(t, d).start()
+        if last:
+            share_copy().start()
+            final = inverse_factor(gram_total)
 
         def drain(c, carry, t=t):
             hop1(t, c).wait_send()
@@ -231,33 +259,39 @@
         lax.fori_loop(0, chunks, drain, 0)
         for d in range(1, ranks):
             scatter(t, d).wait_send()
+        for d in range(1, ranks):
             gather(t, d).wait_recv()
-        for d in range(1, ranks):
-            gather(t, d).wait_send()
         for r in range(ranks):
             acc[r * lines : (r + 1) * lines, :] = full[t, r]
-        factor = inverse_factor(acc[:, width : width + k])
-        sums = dot_full(factor, acc[:, 0:width], 1, 0)
-        if t + 1 < TURNS:
-            set_operand(sums)
-
+        if not last:
+            set_operand(acc[:, 0:width])
+            acc_gram[...] = acc[:, width : width + k]
+
+    sums = dot_full(final, acc[:, 0:width], 1, 0)
     coeffs_out[...] = sums
-    own = dot_full(sums, sums, 1, 1)
-    spect[0] = own
+    factor_out[...] = final
+    spect[0] = dot_full(sums, sums, 1, 1)
     for d in range(1, groups):
         share_spectrum(d).start()
-    per = chunks // groups
-    scaled = factor * scale
-    for i in range(per):
-        for h in range(2):
-            at = (i * 2 + h) * HALF
-            basis_out[:, at : at + HALF] = dot_full(scaled, panel[TURNS - 1, me * per + i, h], 1, 0)
-    value = None
+
+    for d in range(1, ranks):
+        give_gram(d).wait_send()
+        for t in range(TURNS):
+            gather(t, d).wait_send()
+    share_copy().wait()
     for d in range(1, groups):
         share_spectrum(d).wait()
     a = spect[0] + spect[2]
     b = spect[1] + spect[3]
     spectrum_out[...] = (a + b) / batch_total
+
+
+def finish(scale, factor, share, coeffs, spectrum, basis_out, coeffs_out, spectrum_out):
+    scaled = factor[...] * scale
+    for h in range(2):
+        basis_out[:, h * HALF : (h + 1) * HALF] = dot_full(scaled, share[0, h], 1, 0)
+    coeffs_out[...] = coeffs[...]
+    spectrum_out[...] = spectrum[...]
 
 
 def on_device(stress, sketch):
@@ -272,15 +306,17 @@
     scale = math.sqrt(float(rows_dev * ranks))
     vmem = pl.BlockSpec(memory_space=pltpu.VMEM)
     dma = pltpu.SemaphoreType.DMA
-    return pl.pallas_call(
-        functools.partial(kernel, ranks, scale, float(width * groups)),
+    per = chunks // groups
+    part_out, factor, coeffs, spectrum = pl.pallas_call(
+        functools.partial(kernel, ranks, float(width * groups)),
         out_shape=(
-            jax.ShapeDtypeStruct((k, share), F32),
+            jax.ShapeDtypeStruct((per, 2, k, HALF), F32),
+            jax.ShapeDtypeStruct((k, k), F32),
             jax.ShapeDtypeStruct((k, width), F32),
             jax.ShapeDtypeStruct((k, k), F32),
         ),
         in_specs=[pl.BlockSpec(memory_space=pl.ANY), vmem],
-        out_specs=(vmem, vmem, vmem),
+        out_specs=(pl.BlockSpec(memory_space=pl.ANY), vmem, vmem, vmem),
         scratch_shapes=[
             pltpu.VMEM((SLOTS, CHUNK, width), F32),
             pltpu.VMEM((rows_dev, width), BF16),
@@ -297,7 +333,13 @@
             pltpu.VMEM((TURNS, lines, wide), F32),
             pltpu.VMEM((TURNS, ranks, lines, wide), F32),
             pltpu.VMEM((groups, k, k), F32),
+            pltpu.VMEM((k, k), F32),
+            pltpu.VMEM((ranks, k, k), F32),
+            pltpu.VMEM((k, k), F32),
+            pltpu.VMEM((k, k), F32),
+            pltpu.VMEM((chunks, 2, k, HALF), F32),
             dma((SLOTS,)),
+            dma,
             dma((TURNS, chunks)),
             dma((TURNS, chunks)),
             dma((TURNS, chunks)),
@@ -310,6 +352,8 @@
             dma((TURNS, ranks)),
             dma((groups,)),
             dma((groups,)),
+            dma((ranks,)),
+            dma((ranks,)),
         ],
         compiler_params=pltpu.CompilerParams(
             collective_id=0, has_side_effects=True, vmem_limit_bytes=58 * 1024 * 1024
@@ -318,6 +362,27 @@
             flops=24 * rows_dev * width * k, bytes_accessed=rows_dev * width * 4, transcendentals=0
         ),
     )(stress, sketch)
+    same = lambda i: (0, 0)
+    return pl.pallas_call(
+        functools.partial(finish, scale),
+        grid=(per,),
+        out_shape=(
+            jax.ShapeDtypeStruct((k, share), F32),
+            jax.ShapeDtypeStruct((k, width), F32),
+            jax.ShapeDtypeStruct((k, k), F32),
+        ),
+        in_specs=[
+            pl.BlockSpec((k, k), same),
+            pl.BlockSpec((1, 2, k, HALF), lambda i: (i, 0, 0, 0)),
+            pl.BlockSpec((k, width), same),
+            pl.BlockSpec((k, k), same),
+        ],
+        out_specs=(
+            pl.BlockSpec((k, CHUNK), lambda i: (0, i)),
+            pl.BlockSpec((k, width), same),
+            pl.BlockSpec((k, k), same),
+        ),
+    )(factor, part_out, coeffs, spectrum)
 
 
 def solution(mesh):

time: 149 us -> 148 us (level)
  local copies, waits for them, and re-layouts: 5.12 us -> 0 us
  Pallas kernels: 143 us -> 147 us
    unnamed x3 -> x0, local copies, waits for them, and re-layouts: 5.12 us -> none
    pallas_call x1 -> x2, Pallas kernels: 143 us -> 147 us  [the longest x1 143 us: on_device(): pl.pallas_call(functools.partial(kernel, ranks, float(width * groups)), o...]
where the time goes in v2:
time: 148 us; the launch traced here: 147 us
  Pallas kernels  147 us (99%)
    pallas_call x1, Pallas kernels, on_device(): pl.pallas_call(functools.partial(kernel, ranks, float(width * groups)), o...  143 us
    pallas_call x1, Pallas kernels, on_device(): pl.pallas_call(functools.partial(finish, scale), grid=(per,), out_shape=(...  4.09 us

profile of v2, /device:TPU:0, one launch (start us, length us, event | category | flops | bytes accessed | tf_op | source)
XLA Modules:
  0.0 147.4 jit_solution(1197516006856872138)
XLA Ops:
  0.6 142.7 %shard_map.49 = (f32[4,2,64,512]{3,2,1,0:T(8,128)}, f32[64,64]{1,0:T(8,128)}, f32[64,256]{1,0:T(8,128)}, f32[64,64]{1,0:T(8,128)}) custom-call(f32[16384,256]{1,0:T(8,128)} %stress.1, f32[64,256]{1,0:T(8,128)} %sketch.1), custom_call_target="tpu_custom_call" | custom-call | flops 6442450944 | bytes 16777216 | tf_op jit(solution)/shard_map/pallas_call | solution.py:310
  143.3 4.1 %shard_map.50 = (f32[64,4096]{1,0:T(8,128)}, f32[64,256]{1,0:T(8,128)}, f32[64,64]{1,0:T(8,128)}) custom-call(f32[64,64]{1,0:T(8,128)} %get-tuple-element.7.factor, f32[4,2,64,512]{3,2,1,0:T(8,128)} %get-tuple-element.8.share, f32[64,256]{1,0:T(8,128)} %get-tuple-element.9.coeffs, f32[64,64]{1,0:T(8,128)} %get-tuple-element.10.spectrum), custom_call_target="tpu_custom_call" | custom-call | tf_op jit(solution)/shard_map/pallas_call | solution.py:366
